TPU v7x, 256 devices: a whole 4x4x8 slice. The times are simulated.
256 devices in a mesh: doc: 16 (over y, x), cent: 16 (over z, core).
Axes of the slice: x: 4, y: 4, z: 8, core: 2. Of those that a mesh axis runs over, the one named last changes fastest.
Arguments:
- documents: bfloat16 [32768, 768], P('doc'), may hold values from -6 to 6
- centroids: bfloat16 [512, 128, 768], P('cent'), may hold values from -6 to 6
- candidates: int32 [256, 128], P('doc', 'cent'), may hold values from 0 to 31, as said below
- counts: int32 [256, 16], P('doc', 'cent'), may hold values from 1 to 8, as said below
Outputs:
- new_centroids: bfloat16 [512, 128, 768], P('cent', 'doc')
Inputs may be any that keep to these rules, and one draw needn't show every extreme that they name: `candidates`: within one block's list for one index of cent the 8 group numbers are distinct; entries past the live count name some group and are ignored. `counts`: a live count is reached by some block for some index of cent in every draw at its largest value.
All inputs are finite; a program needn't handle non-finite values.
Results may differ from a plain program's by a relative error of at most 0.013.
Values may be sent and summed in bfloat16 or wider, within the bound.
A program may use at most 192 MiB of HBM per device.

v0:
```python
import functools
import math

import jax
import jax.numpy as jnp
from jax import lax
from jax.experimental import pallas as pl
from jax.experimental.pallas import tpu as pltpu
from jax.sharding import PartitionSpec as P

BLOCK = 128
PASSES = 3
SIDE = 4
ORDER = (0, 1, 2, 3, 4)
LAGS = (0, 3, 7, 10, 14)
DIRECT = (16, 11)
UNROLL = (16, 8, 8)

sharpness = 40.0
smoothing = 0.02
prior_weight = 0.05
epsilon = 1e-06

F32 = jnp.float32
BF16 = jnp.bfloat16
MESH = pl.DeviceIdType.MESH


def kernel(
    n_doc,
    n_cent,
    target,
    names_hbm,
    live_hbm,
    docs_hbm,
    cents_hbm,
    out_ref,
    docs,
    cents,
    own_raw,
    own_prior,
    own_rms,
    own_col,
    col_turned,
    kt,
    row_scale,
    column,
    row_send,
    row_recv,
    col_send,
    col_recv,
    parts,
    far_recv,
    near_recv,
    halfway,
    far_recv2,
    near_recv2,
    names_ref,
    live_ref,
    names_rows,
    live_rows,
    place_rows,
    place_ref,
    load_sems,
    row_send_sems,
    row_recv_sems,
    col_send_sems,
    col_recv_sems,
    far_sems,
    near_sems,
    far2_sems,
    near2_sems,
    sent_sems,
    sent2_sems,
):
    groups, group_size, width = cents.shape
    slots, blocks = names_ref.shape

    def cand(b, s):
        return names_ref[s, b]

    def count(b):
        return live_ref[0, b]

    def place(b, g):
        return place_ref[g, b]

    half = width // 2
    d = lax.axis_index("doc")
    c = lax.axis_index("cent")
    x = lax.rem(d, SIDE)
    y = lax.div(d, SIDE)

    doc_step = docs.shape[0] // 4
    cent_step = groups // 8
    doc_loads = [
        pltpu.make_async_copy(
            docs_hbm.at[pl.ds(n * doc_step, doc_step)],
            docs.at[pl.ds(n * doc_step, doc_step)],
            load_sems.at[n],
        )
        for n in range(4)
    ]
    cent_loads = [
        pltpu.make_async_copy(
            cents_hbm.at[pl.ds(n * cent_step, cent_step)],
            cents.at[pl.ds(n * cent_step, cent_step)],
            load_sems.at[4 + n],
        )
        for n in range(8)
    ]
    own_pair = lax.div(d, 2)
    own_load = pltpu.make_async_copy(
        cents_hbm.at[:, pl.ds(pl.multiple_of(own_pair * 16, 16), 16)], own_raw, load_sems.at[12]
    )
    small_loads = [
        pltpu.make_async_copy(src, dst, load_sems.at[14 + n])
        for n, (src, dst) in enumerate(
            (
                (names_hbm, names_rows),
                (live_hbm, live_rows),
                (names_hbm, names_ref),
                (live_hbm, live_ref),
            )
        )
    ]
    for copy in small_loads + cent_loads + doc_loads + [own_load]:
        copy.start()

    barrier = pltpu.get_barrier_semaphore()
    for j in range(1, n_doc):
        pl.semaphore_signal(
            barrier, inc=1, device_id=(lax.rem(d + j, n_doc), c), device_id_type=MESH
        )
    for j in range(1, n_cent):
        pl.semaphore_signal(
            barrier, inc=1, device_id=(d, lax.rem(c + j, n_cent)), device_id_type=MESH
        )

    def unit(values):
        values = values.astype(F32)
        inv = lax.rsqrt(jnp.sum(values * values, axis=-1, keepdims=True) / width + epsilon)
        return values * (inv / math.sqrt(width))

    def unit_cents(n, carry):
        at = pl.ds(n * cent_step, cent_step)
        cents[at] = unit(cents[at]).astype(BF16)
        return carry

    for n in range(8):
        cent_loads[n].wait()
        lax.fori_loop(n, n + 1, unit_cents, 0)
    for copy in small_loads:
        copy.wait()

    zero_tile = blocks * slots
    group_index = lax.broadcasted_iota(jnp.int32, (groups, blocks), 0)
    block_index = lax.broadcasted_iota(jnp.int32, (groups, blocks), 1)
    tiles = jnp.full((groups, blocks), zero_tile, jnp.int32)
    for s in range(slots):
        named = (names_rows[s : s + 1, :] == group_index) & (live_rows[...] > s)
        tiles = jnp.where(named, block_index * slots + s, tiles)
    place_rows[:, :blocks] = tiles
    place_copy = pltpu.make_async_copy(place_rows, place_ref, load_sems.at[13])
    place_copy.start()

    for n in range(4):
        doc_loads[n].wait()

    scale = sharpness * math.log2(math.e)

    def score(b, carry):
        at = pl.ds(pl.multiple_of(b * BLOCK, BLOCK), BLOCK)
        rows = unit(docs[at, :]).astype(BF16)
        docs[at, :] = rows
        picked = jnp.concatenate([cents[cand(b, s)] for s in range(slots)], axis=0)
        cosine = lax.dot_general(
            picked, rows, (((1,), (1,)), ((), ())), preferred_element_type=F32
        )
        total = jnp.zeros((8, BLOCK), F32)
        for s in range(slots):
            shift = jnp.where(s < count(b), F32(-scale), F32(-1e30))
            tile = jnp.exp2(cosine[s * group_size : (s + 1) * group_size] * scale + shift)
            total = total + jnp.sum(tile.reshape(group_size // 8, 8, BLOCK), axis=0)
            kt[b * slots + s] = tile.astype(BF16)
        row_scale[pl.ds(b, 1), :] = jnp.sum(total, axis=0, keepdims=True)
        return carry

    lax.fori_loop(0, blocks, score, 0, unroll=min(blocks, UNROLL[0]))
    kt[blocks * slots] = jnp.zeros((group_size, BLOCK), BF16)

    pl.semaphore_wait(barrier, n_doc - 1 + n_cent - 1)

    def send_rows(n, value):
        row_send[n] = value.astype(row_send.dtype)
        for j in sorted(range(1, n_cent), key=lambda j: -min(j // 2, n_cent // 2 - j // 2)):
            pltpu.make_async_remote_copy(
                src_ref=row_send.at[n],
                dst_ref=row_recv.at[n, j - 1],
                send_sem=row_send_sems.at[n],
                recv_sem=row_recv_sems.at[n],
                device_id=(d, lax.rem(c + j, n_cent)),
                device_id_type=MESH,
            ).start()

    def finish_rows(n):
        whole = row_recv.at[n]
        pltpu.make_async_copy(whole, whole, row_recv_sems.at[n]).wait()
        total = row_send[n].astype(F32)
        for j in range(n_cent - 1):
            total = total + row_recv[n, j].astype(F32)
        row_scale[...] = 1.0 / total

    def send_cols(n, value):
        col_send[n] = value.astype(col_send.dtype)
        for j in sorted(range(1, n_doc), key=lambda j: -(2 - abs(2 - j % 4) + 2 - abs(2 - j // 4))):
            pltpu.make_async_remote_copy(
                src_ref=col_send.at[n],
                dst_ref=col_recv.at[n, j - 1],
                send_sem=col_send_sems.at[n],
                recv_sem=col_recv_sems.at[n],
                device_id=(lax.rem(d + j, n_doc), c),
                device_id_type=MESH,
            ).start()

    def finish_cols(n):
        whole = col_recv.at[n]
        pltpu.make_async_copy(whole, whole, col_recv_sems.at[n]).wait()
        total = col_send[n].astype(F32)
        for j in range(n_doc - 1):
            total = total + col_recv[n, j].astype(F32)
        column[...] = target / (total + smoothing)

    def row_sums():
        row_index = lax.broadcasted_iota(jnp.int32, (blocks, BLOCK), 0)

        def add(b, total):
            pieces = [
                jnp.where(row_index == b, column[pl.ds(cand(b, s), 1), :], 0.0).astype(BF16)
                for s in range(slots)
            ]
            left = jnp.concatenate(pieces, axis=1)
            right = jnp.concatenate([kt[b * slots + s] for s in range(slots)], axis=0)
            return total + jnp.dot(left, right, preferred_element_type=F32)

        return lax.fori_loop(0, blocks, add, jnp.zeros((blocks, BLOCK), F32), unroll=min(blocks, UNROLL[1]))

    def col_sums():
        group_index = lax.broadcasted_iota(jnp.int32, (groups, BLOCK), 0)

        def add(b, total):
            row = row_scale[pl.ds(b, 1), :]
            pieces = [
                jnp.where(group_index == cand(b, s), row, 0.0).astype(BF16)
                for s in range(slots)
            ]
            left = jnp.concatenate(pieces, axis=1)
            right = jnp.concatenate([kt[b * slots + s] for s in range(slots)], axis=1)
            return total + lax.dot_general(
                right, left, (((1,), (1,)), ((), ())), preferred_element_type=F32
            )

        total = lax.fori_loop(0, blocks, add, jnp.zeros((group_size, groups), F32), unroll=min(blocks, UNROLL[2]))
        padded = jnp.concatenate([total, jnp.zeros((group_size, 128 - groups), F32)], axis=1)
        return padded.T[:groups]

    send_rows(0, row_scale[...])

    own_load.wait()
    place_copy.wait()
    odd = lax.rem(d, 2) == 1

    def own_share(g, carry):
        raw = own_raw[g].astype(F32)
        raw = jnp.where(odd, raw[8:], raw[:8])
        mean = jnp.sum(raw * raw, axis=-1, keepdims=True) / width
        inv = lax.rsqrt(mean + epsilon) / math.sqrt(width)
        rounded = (raw * inv).astype(BF16).astype(F32)
        own_prior[g] = prior_weight * rounded
        own_rms[g] = jnp.broadcast_to(jnp.sqrt(mean), (8, 128))
        return carry

    lax.fori_loop(0, groups, own_share, 0)
    finish_rows(0)

    def sweep(n, carry):
        send_cols(n, col_sums())
        finish_cols(n)
        send_rows(n + 1, row_sums())

        @pl.when(n == PASSES - 1)
        def turn():
            padded = jnp.concatenate(
                [column[...], jnp.zeros((128 - groups, group_size), F32)], axis=0
            )
            col_turned[...] = padded.T
            mine = col_turned[pl.ds(pl.multiple_of(d * 8, 8), 8), :]
            for g in range(groups):
                own_col[g] = jnp.broadcast_to(mine[:, g : g + 1], (8, 128))

        finish_rows(n + 1)
        return carry

    lax.fori_loop(0, PASSES, sweep, 0)

    at_x = [y * SIDE + lax.rem(x + j, SIDE) for j in range(SIDE)]
    at_y = [lax.rem(y + j, SIDE) * SIDE + x for j in range(SIDE)]
    rounds = groups // 4

    def copy_to(doc, src, dst, send_sem, recv_sem):
        pltpu.make_async_remote_copy(
            src_ref=src,
            dst_ref=dst,
            send_sem=send_sem,
            recv_sem=recv_sem,
            device_id=(doc, c),
            device_id_type=MESH,
        ).start()

    def ring(q, second):
        along_x = (q == 0) != second
        places, pos = (at_x, x) if along_x else (at_y, y)
        right, left = places[1], places[3]
        return (
            right,
            places[2],
            left,
            pos,
            lax.rem(pos + 1, SIDE),
            lax.rem(pos + 2, SIDE),
            lax.rem(pos + 3, SIDE),
        )

    def weigh(p, q):
        pieces = []
        for gg in range(2):
            pieces.append(
                jnp.concatenate(
                    [
                        (kt[place(b, 2 * p + gg)].astype(F32) * row_scale[b : b + 1, :]).astype(
                            BF16
                        )
                        for b in range(blocks)
                    ],
                    axis=1,
                )
            )
        left = jnp.concatenate(pieces, axis=0)
        total = jnp.dot(left, docs[...], preferred_element_type=F32)
        for dest in range(n_doc):
            dy, dx = dest // SIDE, dest % SIDE
            first, then = (dx, dy) if q == 0 else (dy, dx)
            rows = jnp.concatenate(
                [
                    total[gg * group_size + 8 * dest : gg * group_size + 8 * dest + 8]
                    for gg in range(2)
                ],
                axis=0,
            ).astype(BF16)
            parts[p, first, 0, then] = rows[:, :half]
            parts[p, first, 1, then] = rows[:, half:]

    def leg_start(p, q, second):
        right, across, left, pos, near, far, back = ring(q, second)
        if second:
            piece = lambda place, h: halfway.at[p, h, place]
            far_to, near_to = far_recv2, near_recv2
            far_sem, near_sem, sent = far2_sems.at[p], near2_sems.at[p], sent2_sems.at[p]
        else:
            piece = lambda place, h: parts.at[p, place, h]
            far_to, near_to = far_recv, near_recv
            far_sem, near_sem, sent = far_sems.at[p], near_sems.at[p], sent_sems.at[p]
        @pl.when(p < DIRECT[second])
        def _():
            copy_to(right, piece(far, 0), far_to.at[p, 0], sent, far_sem)
            copy_to(left, piece(far, 1), far_to.at[p, 1], sent, far_sem)

        @pl.when(p >= DIRECT[second])
        def _():
            for h in range(2):
                copy_to(across, piece(far, h), far_to.at[p, h], sent, far_sem)
            copy_to(right, piece(near, 0), near_to.at[p, 0, 0], sent, near_sem)
            copy_to(left, piece(back, 1), near_to.at[p, 1, 1], sent, near_sem)

        copy_to(right, piece(near, 1), near_to.at[p, 0, 1], sent, near_sem)
        copy_to(left, piece(back, 0), near_to.at[p, 1, 0], sent, near_sem)

    def leg_relay(p, q, second):
        right, across, left, pos, near, far, back = ring(q, second)
        if second:
            got, near_to = far_recv2, near_recv2
            far_sem, near_sem, sent = far2_sems.at[p], near2_sems.at[p], sent2_sems.at[p]
        else:
            got, near_to = far_recv, near_recv
            far_sem, near_sem, sent = far_sems.at[p], near_sems.at[p], sent_sems.at[p]
        whole = got.at[p]
        pltpu.make_async_copy(whole, whole, far_sem).wait()
        for h, place, device in ((0, near, right), (1, back, left)):
            if second:
                halfway[p, h, place] = (
                    halfway[p, h, place].astype(F32) + got[p, h].astype(F32)
                ).astype(BF16)
                src = halfway.at[p, h, place]
            else:
                parts[p, place, h] = (
                    parts[p, place, h].astype(F32) + got[p, h].astype(F32)
                ).astype(BF16)
                src = parts.at[p, place, h]
            copy_to(device, src, near_to.at[p, h, h], sent, near_sem)

    def leg_end(p, q, second):
        pos = ring(q, second)[3]
        got = near_recv2 if second else near_recv
        far_got, far_sem = (far_recv2, far2_sems) if second else (far_recv, far_sems)
        near_sem = near2_sems if second else near_sems
        whole = got.at[p]
        pltpu.make_async_copy(whole, whole, near_sem.at[p]).wait()

        @pl.when(p >= DIRECT[second])
        def _():
            whole = far_got.at[p]
            pltpu.make_async_copy(whole, whole, far_sem.at[p]).wait()
            for h in range(2):
                got[p, 0, h] = (got[p, 0, h].astype(F32) + far_got[p, h].astype(F32)).astype(BF16)

        if second:
            return [
                halfway[p, h, pos].astype(F32)
                + near_recv2[p, 0, h].astype(F32)
                + near_recv2[p, 1, h].astype(F32)
                for h in range(2)
            ]
        for h in range(2):
            halfway[p, h] = (
                parts[p, pos, h].astype(F32)
                + near_recv[p, 0, h].astype(F32)
                + near_recv[p, 1, h].astype(F32)
            ).astype(BF16)

    def finish(p, sums):
        for gg in range(2):
            g = 2 * p + gg
            weight = own_col[g][:, :1]
            prior = own_prior[g]
            low = sums[0][8 * gg : 8 * gg + 8] * weight + prior[:, :half]
            high = sums[1][8 * gg : 8 * gg + 8] * weight + prior[:, half:]
            square = jnp.sum(low * low, axis=-1, keepdims=True) + jnp.sum(
                high * high, axis=-1, keepdims=True
            )
            rescale = own_rms[g][:, :1] * lax.rsqrt(square / width + epsilon)
            out_ref[g, :, :half] = (low * rescale).astype(BF16)
            out_ref[g, :, half:] = (high * rescale).astype(BF16)

    pairs = 2 * rounds

    def turn_of(t, q):
        def begin(p, q):
            weigh(p, q)
            leg_start(p, q, False)

        def relay_if(p, q, second):
            @pl.when(p < DIRECT[second])
            def _():
                leg_relay(p, q, second)

        def middle(p, q):
            leg_end(p, q, False)
            leg_start(p, q, True)

        stages = (
            begin,
            lambda p, q: relay_if(p, q, False),
            middle,
            lambda p, q: relay_if(p, q, True),
            lambda p, q: finish(p, leg_end(p, q, True)),
        )
        for n in ORDER:
            lag, step = LAGS[n], stages[n]
            p = t - lag

            @pl.when((p >= 0) & (p < pairs))
            def _(p=p, lag=lag, step=step):
                step(p, (q - lag) % 2)

    def two_turns(u, carry):
        for q in range(2):
            turn_of(2 * u + q, q)
        return carry

    lax.fori_loop(0, (pairs + LAGS[-1] + 1) // 2, two_turns, 0)

    def sent(p, carry):
        whole = parts.at[p, pl.ds(0, 3)]
        pltpu.make_async_copy(whole, whole, sent_sems.at[p]).wait()
        whole = halfway.at[p, :, pl.ds(0, 3)]
        pltpu.make_async_copy(whole, whole, sent2_sems.at[p]).wait()
        return carry

    lax.fori_loop(0, 2 * rounds, sent, 0)
    for n in range(PASSES + 1):
        whole = row_recv.at[n]
        pltpu.make_async_copy(whole, whole, row_send_sems.at[n]).wait()
    for n in range(PASSES):
        whole = col_recv.at[n]
        pltpu.make_async_copy(whole, whole, col_send_sems.at[n]).wait()


def body(n_doc, n_cent, documents, centroids, candidates, counts):
    rows_dev, width = documents.shape
    groups, group_size, unused_width = centroids.shape
    blocks, slots = candidates.shape
    half = width // 2
    pairs = groups // 2
    target = rows_dev * n_doc / (groups * group_size * n_cent)
    names = candidates.T
    live = counts.T
    dma = pltpu.SemaphoreType.DMA
    return pl.pallas_call(
        functools.partial(kernel, n_doc, n_cent, target),
        out_shape=jax.ShapeDtypeStruct((groups, group_size // n_doc, width), BF16),
        in_specs=[pl.BlockSpec(memory_space=pltpu.HBM)] * 4,
        out_specs=pl.BlockSpec(memory_space=pltpu.VMEM),
        scratch_shapes=[
            pltpu.VMEM((rows_dev, width), BF16),
            pltpu.VMEM((groups, group_size, width), BF16),
            pltpu.VMEM((groups, 16, width), BF16),
            pltpu.VMEM((groups, 8, width), F32),
            pltpu.VMEM((groups, 8, 128), F32),
            pltpu.VMEM((groups, 8, 128), F32),
            pltpu.VMEM((128, 128), F32),
            pltpu.VMEM((blocks * slots + 1, group_size, BLOCK), BF16),
            pltpu.VMEM((blocks, BLOCK), F32),
            pltpu.VMEM((groups, group_size), F32),
            pltpu.VMEM((PASSES + 1, blocks, BLOCK), BF16),
            pltpu.VMEM((PASSES + 1, n_cent - 1, blocks, BLOCK), BF16),
            pltpu.VMEM((PASSES, groups, group_size), BF16),
            pltpu.VMEM((PASSES, n_doc - 1, groups, group_size), BF16),
            pltpu.VMEM((pairs, SIDE, 2, SIDE, 16, half), BF16),
            pltpu.VMEM((pairs, 2, SIDE, 16, half), BF16),
            pltpu.VMEM((pairs, 2, 2, SIDE, 16, half), BF16),
            pltpu.VMEM((pairs, 2, SIDE, 16, half), BF16),
            pltpu.VMEM((pairs, 2, 16, half), BF16),
            pltpu.VMEM((pairs, 2, 2, 16, half), BF16),
            pltpu.SMEM((slots, blocks), jnp.int32),
            pltpu.SMEM((1, blocks), jnp.int32),
            pltpu.VMEM((slots, blocks), jnp.int32),
            pltpu.VMEM((1, blocks), jnp.int32),
            pltpu.VMEM((groups, 128), jnp.int32),
            pltpu.SMEM((groups, 128), jnp.int32),
            dma((18,)),
            dma((PASSES + 1,)),
            dma((PASSES + 1,)),
            dma((PASSES,)),
            dma((PASSES,)),
            dma((pairs,)),
            dma((pairs,)),
            dma((pairs,)),
            dma((pairs,)),
            dma((pairs,)),
            dma((pairs,)),
        ],
        compiler_params=pltpu.CompilerParams(
            collective_id=0, has_side_effects=True, vmem_limit_bytes=52 * 1024 * 1024
        ),
    )(names, live, documents, centroids)


def solution(mesh):
    n_doc, n_cent = mesh.shape["doc"], mesh.shape["cent"]
    return jax.shard_map(
        functools.partial(body, n_doc, n_cent),
        mesh=mesh,
        in_specs=(P("doc", None), P("cent", None, None), P("doc", "cent"), P("doc", "cent")),
        out_specs=P("cent", "doc", None),
        check_vma=False,
    )
```

profile of v0, /device:TPU:1, one launch (start us, length us, event | category | flops | bytes accessed | tf_op | source)
XLA Modules:
  0.0 98.1 jit_solution(12884942913576115676)
XLA Ops:
  0.0 0.0 copy-start
  0.0 0.7 copy-done
  0.7 0.0 copy-start.1
  0.7 0.7 copy-done.1
  1.3 96.0 %shard_map.46 = bf16[32,8,768]{2,1,0:T(8,128)(2,1)S(1)} custom-call(s32[8,16]{1,0:T(8,128)S(1)} %bitcast.2, s32[1,16]{1,0:T(1,128)S(1)} %bitcast.3, bf16[2048,768]{1,0:T(8,128)(2,1)} %docs_hbm.1, bf16[32,128,768]{2,1,0:T(8,128)(2,1)} %cents_hbm.1), custom_call_target="tpu_custom_call" | custom-call | tf_op jit(solution)/shard_map/pallas_call | solution.py:518
  97.3 0.7 copy.6
Async XLA Ops:
  0.0 0.7 copy-start
  0.7 0.7 copy-start.1
where the time goes:
time: 98.2 us; the launch traced here: 98.1 us
  Pallas kernels  96 us (98%)
  local copies, waits for them, and re-layouts  2.09 us (2%)
    pallas_call x1, Pallas kernels, body(): pl.pallas_call(functools.partial(kernel, n_doc, n_cent, target), out_shap...  96 us
    unnamed x5, local copies, waits for them, and re-layouts  2.09 us

commit v1 on v0

--- a/solution.py
+++ b/solution.py
@@ -12,7 +12,7 @@
 PASSES = 3
 SIDE = 4
 ORDER = (0, 1, 2, 3, 4)
-LAGS = (0, 3, 7, 10, 14)
+LAGS = (0, 3, 6, 9, 12)
 DIRECT = (16, 11)
 UNROLL = (16, 8, 8)
 
@@ -30,8 +30,7 @@
     n_doc,
     n_cent,
     target,
-    names_hbm,
-    live_hbm,
+    lists_hbm,
     docs_hbm,
     cents_hbm,
     out_ref,
@@ -55,10 +54,8 @@
     halfway,
     far_recv2,
     near_recv2,
-    names_ref,
-    live_ref,
-    names_rows,
-    live_rows,
+    lists_ref,
+    lists_rows,
     place_rows,
     place_ref,
     load_sems,
@@ -74,13 +71,13 @@
     sent2_sems,
 ):
     groups, group_size, width = cents.shape
-    slots, blocks = names_ref.shape
+    slots, blocks = lists_ref.shape[0] - 1, lists_ref.shape[1]
 
     def cand(b, s):
-        return names_ref[s, b]
+        return lists_ref[s, b]
 
     def count(b):
-        return live_ref[0, b]
+        return lists_ref[slots, b]
 
     def place(b, g):
         return place_ref[g, b]
@@ -116,12 +113,7 @@
     small_loads = [
         pltpu.make_async_copy(src, dst, load_sems.at[14 + n])
         for n, (src, dst) in enumerate(
-            (
-                (names_hbm, names_rows),
-                (live_hbm, live_rows),
-                (names_hbm, names_ref),
-                (live_hbm, live_ref),
-            )
+            ((lists_hbm, lists_rows), (lists_hbm, lists_ref))
         )
     ]
     for copy in small_loads + cent_loads + doc_loads + [own_load]:
@@ -142,14 +134,17 @@
         inv = lax.rsqrt(jnp.sum(values * values, axis=-1, keepdims=True) / width + epsilon)
         return values * (inv / math.sqrt(width))
 
+    def cent_load(n):
+        at = pl.ds(n * cent_step, cent_step)
+        return pltpu.make_async_copy(cents_hbm.at[at], cents.at[at], load_sems.at[4 + n])
+
     def unit_cents(n, carry):
         at = pl.ds(n * cent_step, cent_step)
+        cent_load(n).wait()
         cents[at] = unit(cents[at]).astype(BF16)
         return carry
 
-    for n in range(8):
-        cent_loads[n].wait()
-        lax.fori_loop(n, n + 1, unit_cents, 0)
+    lax.fori_loop(0, 8, unit_cents, 0)
     for copy in small_loads:
         copy.wait()
 
@@ -158,7 +153,7 @@
     block_index = lax.broadcasted_iota(jnp.int32, (groups, blocks), 1)
     tiles = jnp.full((groups, blocks), zero_tile, jnp.int32)
     for s in range(slots):
-        named = (names_rows[s : s + 1, :] == group_index) & (live_rows[...] > s)
+        named = (lists_rows[s : s + 1, :] == group_index) & (lists_rows[slots:, :] > s)
         tiles = jnp.where(named, block_index * slots + s, tiles)
     place_rows[:, :blocks] = tiles
     place_copy = pltpu.make_async_copy(place_rows, place_ref, load_sems.at[13])
@@ -467,12 +462,16 @@
             leg_end(p, q, False)
             leg_start(p, q, True)
 
+        def last(p, q):
+            finish(p, leg_end(p, q, True))
+            pair_sent(p)
+
         stages = (
             begin,
             lambda p, q: relay_if(p, q, False),
             middle,
             lambda p, q: relay_if(p, q, True),
-            lambda p, q: finish(p, leg_end(p, q, True)),
+            last,
         )
         for n in ORDER:
             lag, step = LAGS[n], stages[n]
@@ -482,27 +481,27 @@
             def _(p=p, lag=lag, step=step):
                 step(p, (q - lag) % 2)
 
-    def two_turns(u, carry):
-        for q in range(2):
-            turn_of(2 * u + q, q)
-        return carry
-
-    lax.fori_loop(0, (pairs + LAGS[-1] + 1) // 2, two_turns, 0)
-
-    def sent(p, carry):
+    def sums_sent():
+        for n in range(PASSES + 1):
+            whole = row_recv.at[n]
+            pltpu.make_async_copy(whole, whole, row_send_sems.at[n]).wait()
+        for n in range(PASSES):
+            whole = col_recv.at[n]
+            pltpu.make_async_copy(whole, whole, col_send_sems.at[n]).wait()
+
+    def pair_sent(p):
         whole = parts.at[p, pl.ds(0, 3)]
         pltpu.make_async_copy(whole, whole, sent_sems.at[p]).wait()
         whole = halfway.at[p, :, pl.ds(0, 3)]
         pltpu.make_async_copy(whole, whole, sent2_sems.at[p]).wait()
+
+    def two_turns(u, carry):
+        pl.when(u == 1)(sums_sent)
+        for q in range(2):
+            turn_of(2 * u + q, q)
         return carry
 
-    lax.fori_loop(0, 2 * rounds, sent, 0)
-    for n in range(PASSES + 1):
-        whole = row_recv.at[n]
-        pltpu.make_async_copy(whole, whole, row_send_sems.at[n]).wait()
-    for n in range(PASSES):
-        whole = col_recv.at[n]
-        pltpu.make_async_copy(whole, whole, col_send_sems.at[n]).wait()
+    lax.fori_loop(0, (pairs + LAGS[-1] + 1) // 2, two_turns, 0)
 
 
 def body(n_doc, n_cent, documents, centroids, candidates, counts):
@@ -512,13 +511,12 @@
     half = width // 2
     pairs = groups // 2
     target = rows_dev * n_doc / (groups * group_size * n_cent)
-    names = candidates.T
-    live = counts.T
+    lists = jnp.concatenate([candidates.T, counts.T], axis=0)
     dma = pltpu.SemaphoreType.DMA
     return pl.pallas_call(
         functools.partial(kernel, n_doc, n_cent, target),
         out_shape=jax.ShapeDtypeStruct((groups, group_size // n_doc, width), BF16),
-        in_specs=[pl.BlockSpec(memory_space=pltpu.HBM)] * 4,
+        in_specs=[pl.BlockSpec(memory_space=pltpu.HBM)] * 3,
         out_specs=pl.BlockSpec(memory_space=pltpu.VMEM),
         scratch_shapes=[
             pltpu.VMEM((rows_dev, width), BF16),
@@ -541,10 +539,8 @@
             pltpu.VMEM((pairs, 2, SIDE, 16, half), BF16),
             pltpu.VMEM((pairs, 2, 16, half), BF16),
             pltpu.VMEM((pairs, 2, 2, 16, half), BF16),
-            pltpu.SMEM((slots, blocks), jnp.int32),
-            pltpu.SMEM((1, blocks), jnp.int32),
-            pltpu.VMEM((slots, blocks), jnp.int32),
-            pltpu.VMEM((1, blocks), jnp.int32),
+            pltpu.SMEM((slots + 1, blocks), jnp.int32),
+            pltpu.VMEM((slots + 1, blocks), jnp.int32),
             pltpu.VMEM((groups, 128), jnp.int32),
             pltpu.SMEM((groups, 128), jnp.int32),
             dma((18,)),
@@ -562,7 +558,7 @@
         compiler_params=pltpu.CompilerParams(
             collective_id=0, has_side_effects=True, vmem_limit_bytes=52 * 1024 * 1024
         ),
-    )(names, live, documents, centroids)
+    )(lists, documents, centroids)
 
 
 def solution(mesh):

time: 98.2 us -> 97.3 us (level)
  local copies, waits for them, and re-layouts: 2.09 us -> 0.75 us
    unnamed x5 -> x1, local copies, waits for them, and re-layouts: 2.09 us -> 0.75 us
where the time goes in v1:
time: 97.3 us; the launch traced here: 97.1 us
  Pallas kernels  95.7 us (98%)
    pallas_call x1, Pallas kernels, body(): pl.pallas_call(functools.partial(kernel, n_doc, n_cent, target), out_shap...  95.7 us

profile of v1, /device:TPU:1, one launch (start us, length us, event | category | flops | bytes accessed | tf_op | source)
XLA Modules:
  0.0 97.1 jit_solution(15269909241479495778)
XLA Ops:
  0.0 0.7 pad_add_fusion.lists_hbm
  0.7 95.7 %shard_map.46 = bf16[32,8,768]{2,1,0:T(8,128)(2,1)S(1)} custom-call(s32[9,16]{1,0:T(8,128)S(1)} %pad_add_fusion.lists_hbm, bf16[2048,768]{1,0:T(8,128)(2,1)} %docs_hbm.1, bf16[32,128,768]{2,1,0:T(8,128)(2,1)} %cents_hbm.1), custom_call_target="tpu_custom_call" | custom-call | tf_op jit(solution)/shard_map/pallas_call | solution.py:516
  96.4 0.7 copy.6
